TPU v7x, 32 devices: a whole 2x2x4 slice. The times are simulated.
32 devices in a mesh: chan: 8 (over y, x, core), seg: 4 (over z).
Axes of the slice: x: 2, y: 2, z: 4, core: 2. Of those that a mesh axis runs over, the one named last changes fastest.
Arguments:
- traces: bfloat16 [16, 1024, 1792], P('seg', 'chan'), may hold values from -6 to 6
- live_first: int32 [8], P('chan'), may hold values from 0 to 32
- live_end: int32 [8], P('chan'), may hold values from 96 to 128
- tile_owner: int32 [8, 12], replicated, may hold values from 0 to 7, as said below
Outputs:
- cross_stacks: bfloat16 [8, 24, 2, 128, 4096], P('chan', None, None, 'seg')
Inputs may be any that keep to these rules, and one draw needn't show every extreme that they name: The 12 tiles of one row block r (tile_owner[r, :]) go to 4 different owners, 3 to each, in an order drawn from the seed. No owner takes more than 24 tiles in all, and one owner takes exactly 24.
All inputs are finite; a program needn't handle non-finite values.
Results may differ from a plain program's by a relative error of at most 0.0068.
Values may be sent and summed in bfloat16 or wider, within the bound.
A program may use at most 128 MiB of HBM per device.

v0:
```python
from functools import partial
import math

import jax
import jax.numpy as jnp
from jax import lax
from jax.sharding import PartitionSpec as P

SAMPLES = 1792
BINS = 128
F_LOW = 20
SMOOTH = 64
TILES = 3
ROW_PARTS = 4


EPSILON = 1e-06


def from_behind(value, axis, by):
    count = lax.axis_size(axis)
    pairs = [(i, i + by) for i in range(count) if 0 <= i + by < count]
    return lax.ppermute(value, axis, pairs)


def build_table(piece_count):
    bins_here = BINS // piece_count
    sample_idx = jnp.arange(SAMPLES, dtype=jnp.int32)
    column = jnp.arange(2 * BINS, dtype=jnp.int32)
    piece = column // (2 * bins_here)
    part_index = column // bins_here % 2
    within = column % bins_here
    frequency = F_LOW + piece * bins_here + within
    phase = sample_idx[:, None] * frequency[None, :] % SAMPLES
    angle = 2.0 * math.pi / SAMPLES * phase.astype(jnp.float32)
    taper = 0.5 - 0.5 * jnp.cos(2.0 * math.pi / SAMPLES * (sample_idx.astype(jnp.float32) + 0.5))
    wave = jnp.where(part_index[None, :] == 0, jnp.cos(angle), -jnp.sin(angle))
    return (taper[:, None] * wave).astype(jnp.bfloat16)


def window_matrix():
    bin_from = jnp.arange(BINS, dtype=jnp.int32)[:, None]
    bin_to = jnp.arange(BINS, dtype=jnp.int32)[None, :]
    first_bin = jnp.clip(bin_to - SMOOTH // 2, 0, BINS - SMOOTH)
    inside = (bin_from >= first_bin) & (bin_from < first_bin + SMOOTH)
    return jnp.where(inside, 1.0 / SMOOTH, 0.0).astype(jnp.float32)


def cross_stack(banded, row_width):
    row_part = banded[..., :row_width]
    col_part = banded[..., row_width:]
    flipped = jnp.stack([row_part[:, :, 1], -row_part[:, :, 0]], axis=2)
    paired = jnp.stack([row_part, flipped], axis=1)
    result = jnp.einsum("kaspfi,kspfj->kafij", paired, col_part, preferred_element_type=jnp.float32)
    result = (result * (1.0 / banded.shape[1])).astype(jnp.bfloat16)
    return result.reshape(banded.shape[0], 2, banded.shape[3], row_width * col_part.shape[-1])


def pick_rows(table, source_index, valid):
    taken = jnp.take(table, source_index, axis=0)
    keep = valid.reshape((valid.shape[0],) + (1,) * (table.ndim - 1))
    return jnp.where(keep, taken, jnp.zeros_like(taken))


def band_inputs(whitened):
    seg_total = whitened.shape[0]
    bins_here = whitened.shape[2]
    block_width = whitened.shape[3]
    part_rows = block_width // ROW_PARTS
    columns = [whitened]
    for step in range(1, TILES):
        columns.append(from_behind(whitened, "chan", -step))
    columns = jnp.stack(columns, axis=0)
    row_blocks = whitened.reshape(seg_total, 2, bins_here, ROW_PARTS, part_rows)
    row_blocks = jnp.transpose(row_blocks, (3, 0, 1, 2, 4))
    row_blocks = jnp.broadcast_to(row_blocks[None], (TILES,) + row_blocks.shape)
    columns = jnp.broadcast_to(columns[:, None], (TILES, ROW_PARTS) + columns.shape[1:])
    banded = jnp.concatenate([row_blocks, columns], axis=-1)
    return banded.reshape((TILES * ROW_PARTS,) + banded.shape[2:])


def per_device(traces, live_first, live_end, tile_owner):
    chan_count = lax.axis_size("chan")
    seg_count = lax.axis_size("seg")
    block_width = traces.shape[1]
    segs_here = traces.shape[0]
    bins_here = BINS // seg_count
    part_rows = block_width // ROW_PARTS
    spectra = jnp.einsum(
        "sct,tq->sqc", traces, build_table(seg_count), preferred_element_type=jnp.float32
    )
    spectra = spectra.reshape(segs_here, seg_count, 2, bins_here, block_width)
    powers = (spectra[:, :, 0] * spectra[:, :, 0] + spectra[:, :, 1] * spectra[:, :, 1]).reshape(
        segs_here, BINS, block_width
    )
    smoothed = jnp.einsum("sgc,gf->sfc", powers, window_matrix(), precision=lax.Precision.HIGHEST)
    scaling = (1.0 / jnp.sqrt(smoothed + EPSILON)).reshape(
        segs_here, seg_count, 1, bins_here, block_width
    )
    channel_offset = jnp.arange(block_width, dtype=jnp.int32)
    live_mask = ((channel_offset >= live_first[0]) & (channel_offset < live_end[0])).astype(
        jnp.float32
    )
    whitened = (spectra * scaling * live_mask).astype(jnp.bfloat16)
    whitened = lax.all_to_all(whitened, "seg", split_axis=1, concat_axis=0, tiled=True)
    seg_total = whitened.shape[0]
    whitened = whitened.reshape(seg_total, 2, bins_here, block_width)
    my_index = lax.axis_index("chan")
    banded = band_inputs(whitened)
    item_count = tile_owner.shape[1]
    my_owners = lax.dynamic_slice_in_dim(tile_owner, my_index, 1, 0).reshape(-1)
    per_link = max(1, item_count // (chan_count // 2))
    place_count = chan_count * per_link
    local_ids = jnp.arange(item_count, dtype=jnp.int32)
    earlier = local_ids[None, :] < local_ids[:, None]
    order_rank = jnp.sum(
        ((my_owners[:, None] == my_owners[None, :]) & earlier).astype(jnp.int32), axis=1
    )
    place_ids = jnp.arange(place_count, dtype=jnp.int32)
    place_owner = place_ids // per_link
    place_rank = place_ids % per_link
    send_hit = (my_owners[None, :] == place_owner[:, None]) & (
        order_rank[None, :] == place_rank[:, None]
    )
    send_index = jnp.sum(send_hit.astype(jnp.int32) * local_ids[None, :], axis=1)
    send_valid = jnp.any(send_hit, axis=1)
    outgoing = pick_rows(banded, send_index, send_valid)
    outgoing = outgoing.reshape(
        chan_count, per_link, seg_total, 2, bins_here, part_rows + block_width
    )
    arrived = lax.all_to_all(outgoing, "chan", split_axis=0, concat_axis=0, tiled=True)
    sources = arrived.shape[0]
    arrived_count = arrived.shape[1]
    grouped = arrived.reshape((4, sources * arrived_count // 4) + arrived.shape[2:])
    result = lax.map(partial(cross_stack, row_width=part_rows), grouped)
    received = result.reshape(sources, arrived_count, 2, bins_here, part_rows * block_width)
    received = received.reshape(place_count, 2, bins_here, part_rows * block_width)
    from_each = jnp.sum((tile_owner == my_index).astype(jnp.int32), axis=1)
    filled = (place_rank < from_each[place_owner]).astype(jnp.int32)
    filled_rank = jnp.cumsum(filled) - filled
    slot_count = 2 * item_count
    slot_ids = jnp.arange(slot_count, dtype=jnp.int32)
    keep_hit = (filled[None, :] == 1) & (filled_rank[None, :] == slot_ids[:, None])
    keep_index = jnp.sum(keep_hit.astype(jnp.int32) * place_ids[None, :], axis=1)
    keep_valid = jnp.any(keep_hit, axis=1)
    packed = pick_rows(received, keep_index, keep_valid)
    return packed.reshape(1, slot_count, 2, bins_here, part_rows * block_width)


def solution(mesh):
    placed = (P("seg", "chan", None), P("chan"), P("chan"), P())
    return jax.shard_map(
        per_device,
        mesh=mesh,
        in_specs=placed,
        out_specs=P("chan", None, None, "seg", None),
        check_vma=False,
    )
```

profile of v0, /device:TPU:0, one launch (start us, length us, event | category | flops | bytes accessed | tf_op | source)
XLA Modules:
  0.0 301.2 jit_solution(8025170435839629555)
XLA Ops:
  1.5 8.0 %fusion.17 = f32[256,4,128]{2,0,1:T(8,128)S(1)} fusion(bf16[4,128,1792]{2,1,0:T(8,128)(2,1)S(1)} %copy-done, s32[256]{0:T(256)S(1)} %fusion.42, f32[1792]{0:T(1024)S(1)} %multiply_subtract_fusion, pred[256]{0:T(512)(128)(4,1)S(1)} %fusion.47), kind=kOutput, calls=%fused_computation.32 | convolution fusion | flops 475725824 | bytes 2367744 | tf_op jit(solution)/shard_map/sct,tq->sqc/dot_general | solution.py:89
  12.1 6.3 %all-to-all-start = ((bf16[4,4,2,32,128]{4,3,2,0,1:T(8,128)(2,1)}), bf16[4,4,2,32,128]{4,3,2,0,1:T(8,128)(2,1)S(1)}, u32[]{:S(2)}, u32[]{:S(2)}) async-start(bf16[4,4,2,32,128]{4,3,2,0,1:T(8,128)(2,1)} %fusion.26), calls=%async_computation | async-start | bytes 524288 | tf_op jit(solution)/shard_map/all_to_all | solution.py:105
  18.9 8.5 %all-to-all-done = bf16[4,4,2,32,128]{4,3,2,0,1:T(8,128)(2,1)S(1)} async-done(((bf16[4,4,2,32,128]{4,3,2,0,1:T(8,128)(2,1)}), bf16[4,4,2,32,128]{4,3,2,0,1:T(8,128)(2,1)S(1)}, u32[]{:S(2)}, u32[]{:S(2)}) %all-to-all-start) | async-done | bytes 262176 | tf_op jit(solution)/shard_map/all_to_all | solution.py:105
  31.0 9.7 %collective-permute-done.1 = bf16[16,2,32,128]{3,2,1,0:T(8,128)(2,1)S(1)} collective-permute-done((bf16[16,2,32,128]{3,2,1,0:T(8,128)(2,1)S(1)}, bf16[16,2,32,128]{3,2,1,0:T(8,128)(2,1)S(1)}, u32[]{:S(2)}, u32[]{:S(2)}) %collective-permute-start.1) | collective-permute-done | bytes 262176 | tf_op jit(solution)/shard_map/ppermute | solution.py:23
  42.4 5.4 %pad_maximum_fusion = bf16[3,4,16,2,32,160]{5,4,3,2,1,0:T(8,128)(2,1)} fusion(bf16[3,4,16,2,32,128]{5,4,3,2,1,0:T(8,128)(2,1)S(1)} %broadcast_in_dim.107, bf16[3,4,16,2,32,32]{5,4,3,2,1,0:T(8,128)(2,1)S(1)} %broadcast_in_dim.106), kind=kLoop, calls=%fused_computation.20 | loop fusion | flops 7864320 | bytes 7864320 | tf_op jit(solution)/shard_map/concatenate | solution.py:78
  47.8 8.9 %gather_fusion.1 = bf16[24,16,2,32,160]{4,3,2,1,0:T(8,128)(2,1)} fusion(bf16[12,16,2,32,160]{4,3,2,1,0:T(8,128)(2,1)} %bitcast.93, s32[1024]{0:T(1024)S(1)} %pad_clamp_fusion.1), kind=kCustom, calls=%fused_computation.1 | custom fusion | bytes 15728736 | tf_op jit(solution)/shard_map/jit(_take)/gather | solution.py:60
  56.7 10.9 %select_select_fusion = bf16[8,3,16,2,32,160]{5,4,3,2,1,0:T(8,128)(2,1)} fusion(bf16[8,3,16,2,32,160]{5,4,3,2,1,0:T(8,128)(2,1)} %bitcast.94, pred[8,3]{1,0:T(8,128)(4,1)S(1)} %compare_and_fusion.1, pred[8,3]{1,0:T(8,128)(4,1)S(1)} %broadcast_in_dim.100), kind=kLoop, calls=%fused_computation.19 | loop fusion | flops 7864320 | bytes 15728688 | tf_op jit(solution)/shard_map/jit(_where)/select_n | solution.py:62
  67.6 5.6 %all-to-all-start.1 = ((bf16[8,3,16,2,32,160]{5,4,3,2,1,0:T(8,128)(2,1)}), bf16[8,3,16,2,32,160]{5,4,3,2,1,0:T(8,128)(2,1)}, u32[]{:S(2)}, u32[]{:S(2)}) async-start(bf16[8,3,16,2,32,160]{5,4,3,2,1,0:T(8,128)(2,1)} %select_select_fusion), calls=%async_computation.1 | async-start | bytes 25165824 | tf_op jit(solution)/shard_map/all_to_all | solution.py:131
  74.6 137.4 %all-to-all-done.1 = bf16[8,3,16,2,32,160]{5,4,3,2,1,0:T(8,128)(2,1)} async-done(((bf16[8,3,16,2,32,160]{5,4,3,2,1,0:T(8,128)(2,1)}), bf16[8,3,16,2,32,160]{5,4,3,2,1,0:T(8,128)(2,1)}, u32[]{:S(2)}, u32[]{:S(2)}) %all-to-all-start.1) | async-done | bytes 7864352 | tf_op jit(solution)/shard_map/all_to_all | solution.py:131
  212.0 14.0 %copy.20 = bf16[8,3,16,2,32,160]{5,2,3,4,1,0:T(8,128)(2,1)} copy(bf16[8,3,16,2,32,160]{5,4,3,2,1,0:T(8,128)(2,1)} %all-to-all-done.1) | data formatting | bytes 15728640 | tf_op jit(solution)/shard_map/all_to_all | solution.py:131
  226.0 53.9 %while.10 = (s32[]{:T(128)}, bf16[4,6,2,32,4096]{4,3,2,1,0:T(8,128)(2,1)}, bf16[4,6,16,2,32,160]{5,2,3,4,1,0:T(8,128)(2,1)}, s32[]{:T(128)}) while((s32[]{:T(128)}, bf16[4,6,2,32,4096]{4,3,2,1,0:T(8,128)(2,1)}, bf16[4,6,16,2,32,160]{5,2,3,4,1,0:T(8,128)(2,1)}, s32[]{:T(128)}) %tuple.29), condition=%wide.region_8.9_spmd, body=%wide.region_7.8_spmd.sunk | while | flops 105676800 | bytes 26739256 | solution.py:135
  228.7 3.2 %fusion.66 = bf16[6,2,32,32,128]{4,3,1,2,0:T(8,128)(2,1)} fusion(bf16[6,1,16,2,32,32]{5,2,3,1,4,0:T(8,128)(2,1)S(1)} %get-tuple-element.62, bf16[6,1,16,2,32,32]{5,2,3,1,4,0:T(8,128)(2,1)S(1)} %get-tuple-element.63, bf16[6,16,2,32,160]{4,1,2,3,0:T(8,128)(2,1)S(1)} %dynamic-slice_bitcast_fusion.3), kind=kOutput, calls=%fused_computation.5.clone.1 | convolution fusion | flops 105381888 | bytes 7864320 | tf_op jit(solution)/shard_map/while/body/eval_jaxpr/kaspfi,kspfj->kafij/dot_general | solution.py:54
  231.9 3.7 %broadcast_in_dim.133 = bf16[1,6,2,32,4096]{4,2,3,1,0:T(2,128)(2,1)S(1)} reshape(bf16[6,2,32,32,128]{4,3,1,2,0:T(8,128)(2,1)} %fusion.66) | data formatting | bytes 6291456 | tf_op jit(solution)/shard_map/while/body/jit(dynamic_update_index_in_dim)/broadcast_in_dim | solution.py:135
  235.7 3.8 %copy_dynamic-update-slice_fusion.2 = bf16[4,6,2,32,4096]{4,3,2,1,0:T(8,128)(2,1)} fusion(bf16[4,6,2,32,4096]{4,3,2,1,0:T(8,128)(2,1)} %get-tuple-element.69, s32[]{:T(128)} %get-tuple-element.68, bf16[1,6,2,32,4096]{4,2,3,1,0:T(2,128)(2,1)S(1)} %broadcast_in_dim.133), kind=kLoop, calls=%fused_computation.10.clone.1 | loop fusion | bytes 6291968 | tf_op jit(solution)/shard_map/while/body/jit(dynamic_update_index_in_dim)/dynamic_update_slice | solution.py:135
  242.2 3.2 %fusion.66 = bf16[6,2,32,32,128]{4,3,1,2,0:T(8,128)(2,1)} fusion(bf16[6,1,16,2,32,32]{5,2,3,1,4,0:T(8,128)(2,1)S(1)} %get-tuple-element.62, bf16[6,1,16,2,32,32]{5,2,3,1,4,0:T(8,128)(2,1)S(1)} %get-tuple-element.63, bf16[6,16,2,32,160]{4,1,2,3,0:T(8,128)(2,1)S(1)} %dynamic-slice_bitcast_fusion.3), kind=kOutput, calls=%fused_computation.5.clone.1 | convolution fusion | flops 105381888 | bytes 7864320 | tf_op jit(solution)/shard_map/while/body/eval_jaxpr/kaspfi,kspfj->kafij/dot_general | solution.py:54
  245.4 3.7 %broadcast_in_dim.133 = bf16[1,6,2,32,4096]{4,2,3,1,0:T(2,128)(2,1)S(1)} reshape(bf16[6,2,32,32,128]{4,3,1,2,0:T(8,128)(2,1)} %fusion.66) | data formatting | bytes 6291456 | tf_op jit(solution)/shard_map/while/body/jit(dynamic_update_index_in_dim)/broadcast_in_dim | solution.py:135
  249.1 3.8 %copy_dynamic-update-slice_fusion.2 = bf16[4,6,2,32,4096]{4,3,2,1,0:T(8,128)(2,1)} fusion(bf16[4,6,2,32,4096]{4,3,2,1,0:T(8,128)(2,1)} %get-tuple-element.69, s32[]{:T(128)} %get-tuple-element.68, bf16[1,6,2,32,4096]{4,2,3,1,0:T(2,128)(2,1)S(1)} %broadcast_in_dim.133), kind=kLoop, calls=%fused_computation.10.clone.1 | loop fusion | bytes 6291968 | tf_op jit(solution)/shard_map/while/body/jit(dynamic_update_index_in_dim)/dynamic_update_slice | solution.py:135
  255.7 3.2 %fusion.66 = bf16[6,2,32,32,128]{4,3,1,2,0:T(8,128)(2,1)} fusion(bf16[6,1,16,2,32,32]{5,2,3,1,4,0:T(8,128)(2,1)S(1)} %get-tuple-element.62, bf16[6,1,16,2,32,32]{5,2,3,1,4,0:T(8,128)(2,1)S(1)} %get-tuple-element.63, bf16[6,16,2,32,160]{4,1,2,3,0:T(8,128)(2,1)S(1)} %dynamic-slice_bitcast_fusion.3), kind=kOutput, calls=%fused_computation.5.clone.1 | convolution fusion | flops 105381888 | bytes 7864320 | tf_op jit(solution)/shard_map/while/body/eval_jaxpr/kaspfi,kspfj->kafij/dot_general | solution.py:54
  258.8 3.7 %broadcast_in_dim.133 = bf16[1,6,2,32,4096]{4,2,3,1,0:T(2,128)(2,1)S(1)} reshape(bf16[6,2,32,32,128]{4,3,1,2,0:T(8,128)(2,1)} %fusion.66) | data formatting | bytes 6291456 | tf_op jit(solution)/shard_map/while/body/jit(dynamic_update_index_in_dim)/broadcast_in_dim | solution.py:135
  262.6 3.8 %copy_dynamic-update-slice_fusion.2 = bf16[4,6,2,32,4096]{4,3,2,1,0:T(8,128)(2,1)} fusion(bf16[4,6,2,32,4096]{4,3,2,1,0:T(8,128)(2,1)} %get-tuple-element.69, s32[]{:T(128)} %get-tuple-element.68, bf16[1,6,2,32,4096]{4,2,3,1,0:T(2,128)(2,1)S(1)} %broadcast_in_dim.133), kind=kLoop, calls=%fused_computation.10.clone.1 | loop fusion | bytes 6291968 | tf_op jit(solution)/shard_map/while/body/jit(dynamic_update_index_in_dim)/dynamic_update_slice | solution.py:135
  272.3 3.7 %broadcast_in_dim.133 = bf16[1,6,2,32,4096]{4,2,3,1,0:T(2,128)(2,1)S(1)} reshape(bf16[6,2,32,32,128]{4,3,1,2,0:T(8,128)(2,1)} %fusion.66) | data formatting | bytes 6291456 | tf_op jit(solution)/shard_map/while/body/jit(dynamic_update_index_in_dim)/broadcast_in_dim | solution.py:135
  276.0 3.8 %copy_dynamic-update-slice_fusion.2 = bf16[4,6,2,32,4096]{4,3,2,1,0:T(8,128)(2,1)} fusion(bf16[4,6,2,32,4096]{4,3,2,1,0:T(8,128)(2,1)} %get-tuple-element.69, s32[]{:T(128)} %get-tuple-element.68, bf16[1,6,2,32,4096]{4,2,3,1,0:T(2,128)(2,1)S(1)} %broadcast_in_dim.133), kind=kLoop, calls=%fused_computation.10.clone.1 | loop fusion | bytes 6291968 | tf_op jit(solution)/shard_map/while/body/jit(dynamic_update_index_in_dim)/dynamic_update_slice | solution.py:135
  279.8 10.4 %gather_fusion.2 = bf16[24,2,32,4096]{3,2,1,0:T(8,128)(2,1)} fusion(bf16[24,2,32,4096]{3,2,1,0:T(8,128)(2,1)} %bitcast.95, s32[1024]{0:T(1024)S(1)} %pad_clamp_fusion), kind=kCustom, calls=%fused_computation.2 | custom fusion | bytes 25165920 | tf_op jit(solution)/shard_map/jit(_take)/gather | solution.py:60
  290.2 11.0 %fusion.9 = bf16[1,24,2,32,4096]{4,3,2,1,0:T(8,128)(2,1)} fusion(bf16[24,2,32,4096]{3,2,1,0:T(8,128)(2,1)} %gather_fusion.2, pred[24]{0:T(512)(128)(4,1)S(1)} %compare_and_fusion.2, pred[24]{0:T(512)(128)(4,1)S(1)} %fusion.37), kind=kLoop, calls=%fused_computation.18 | loop fusion | flops 12582912 | bytes 25165872 | tf_op jit(solution)/shard_map/jit(_where)/select_n | solution.py:62
  (61 shorter events, 23.9 us)
Async XLA Ops:
  0.0 1.5 copy-start
  1.5 17.0 %copy-start.2 = (s32[8,12]{1,0:T(8,128)S(1)}, s32[8,12]{1,0:T(8,128)}, u32[]{:S(2)}) copy-start(s32[8,12]{1,0:T(8,128)} %param.9) | copy-start | bytes 1156
  12.1 15.2 %all-to-all-start = ((bf16[4,4,2,32,128]{4,3,2,0,1:T(8,128)(2,1)}), bf16[4,4,2,32,128]{4,3,2,0,1:T(8,128)(2,1)S(1)}, u32[]{:S(2)}, u32[]{:S(2)}) async-start(bf16[4,4,2,32,128]{4,3,2,0,1:T(8,128)(2,1)} %fusion.26), calls=%async_computation | async-start | bytes 524288 | tf_op jit(solution)/shard_map/all_to_all | solution.py:105
  27.4 3.6 %collective-permute-start = (bf16[16,2,32,128]{3,2,1,0:T(8,128)(2,1)S(1)}, bf16[16,2,32,128]{3,2,1,0:T(8,128)(2,1)S(1)}, u32[]{:S(2)}, u32[]{:S(2)}) collective-permute-start(bf16[16,2,32,128]{3,2,1,0:T(8,128)(2,1)S(1)} %bitcast.97), channel_id=1, source_target_pairs={{4,0},{8,4},{12,8},{16,12},{20,16},{24,20},{28,24},{5,1},{9,5},{13... | collective-permute-start | bytes 786440 | tf_op jit(solution)/shard_map/ppermute | solution.py:23
  28.7 12.1 %collective-permute-start.1 = (bf16[16,2,32,128]{3,2,1,0:T(8,128)(2,1)S(1)}, bf16[16,2,32,128]{3,2,1,0:T(8,128)(2,1)S(1)}, u32[]{:S(2)}, u32[]{:S(2)}) collective-permute-start(bf16[16,2,32,128]{3,2,1,0:T(8,128)(2,1)S(1)} %bitcast.98), channel_id=1, source_target_pairs={{8,0},{12,4},{16,8},{20,12},{24,16},{28,20},{9,1},{13,5},{17,9},{2... | collective-permute-start | bytes 786440 | tf_op jit(solution)/shard_map/ppermute | solution.py:23
  67.6 144.4 %all-to-all-start.1 = ((bf16[8,3,16,2,32,160]{5,4,3,2,1,0:T(8,128)(2,1)}), bf16[8,3,16,2,32,160]{5,4,3,2,1,0:T(8,128)(2,1)}, u32[]{:S(2)}, u32[]{:S(2)}) async-start(bf16[8,3,16,2,32,160]{5,4,3,2,1,0:T(8,128)(2,1)} %select_select_fusion), calls=%async_computation.1 | async-start | bytes 25165824 | tf_op jit(solution)/shard_map/all_to_all | solution.py:131
  290.2 11.0 %copy-start.1 = (bf16[4,128,1792]{2,1,0:T(8,128)(2,1)S(1)}, bf16[4,128,1792]{2,1,0:T(8,128)(2,1)}, u32[]{:S(2)}) copy-start(bf16[4,128,1792]{2,1,0:T(8,128)(2,1)} %param.6) | copy-start | bytes 5505028
where the time goes:
time: 302 us; the launch traced here: 301 us
  waiting for transfers between devices  156 us (52%)
  local copies, waits for them, and re-layouts  76.9 us (25%)
  other arithmetic  31.4 us (10%)
  matrix products  21.1 us (7%)
  starting transfers between devices  14.7 us (5%)
    all_to_all x1, waiting for transfers between devices, per_device(): lax.all_to_all(outgoing, 'chan', split_axis=0, concat_axis=0, tiled=True)  137 us
    select_n x2, other arithmetic, pick_rows(): return jnp.where(keep, taken, jnp.zeros_like(taken))  21.9 us
    gather x2, local copies, waits for them, and re-layouts, pick_rows(): taken = jnp.take(table, source_index, axis=0)  19.3 us
    dynamic_update_slice x4, local copies, waits for them, and re-layouts, per_device(): result = lax.map(partial(cross_stack, row_width=part_rows), grouped)  15.2 us
    broadcast_in_dim x4, local copies, waits for them, and re-layouts, per_device(): result = lax.map(partial(cross_stack, row_width=part_rows), grouped)  15 us
    all_to_all x1, local copies, waits for them, and re-layouts, per_device(): lax.all_to_all(outgoing, 'chan', split_axis=0, concat_axis=0, tiled=True)  14 us
    dot_general x4, matrix products, cross_stack(): jnp.einsum('kaspfi,kspfj->kafij', paired, col_part, preferred_element_typ...  12.7 us
    ppermute x2, waiting for transfers between devices, from_behind(): return lax.ppermute(value, axis, pairs)  9.7 us
  transfers between devices with their start and end apart: 4, of which 3 were waited for; matrix products, arithmetic and copies ran while one was open for 1% of the time, Pallas kernels for 0%

commit v1 on v0

v1 whole, which is shorter than its diff:
```python
from functools import partial
import math

import jax
import jax.numpy as jnp
import ml_dtypes
import numpy as np
from jax import lax
from jax.experimental import pallas as pl
from jax.experimental.pallas import tpu as pltpu
from jax.sharding import PartitionSpec as P

SAMPLES = 1792
BINS = 128
F_LOW = 20
SMOOTH = 64
TILES = 3
ROW_PARTS = 4
EPSILON = 1e-06
SUB = 8
MESH = pl.DeviceIdType.MESH


def wave_rows():
    t = np.arange(SAMPLES, dtype=np.int64)
    row = np.arange(2 * BINS)
    bin_of = row // (2 * SUB) * SUB + row % SUB
    part = row // SUB % 2
    phase = (t[None, :] * (F_LOW + bin_of)[:, None]) % SAMPLES
    angle = 2.0 * math.pi / SAMPLES * phase
    taper = 0.5 - 0.5 * np.cos(2.0 * math.pi / SAMPLES * (t + 0.5))
    wave = np.where(part[:, None] == 0, np.cos(angle), -np.sin(angle))
    return (taper[None, :] * wave).astype(np.float32).astype(ml_dtypes.bfloat16)


def window_rows():
    to = np.arange(BINS)[:, None]
    frm = np.arange(BINS)[None, :]
    first = np.clip(to - SMOOTH // 2, 0, BINS - SMOOTH)
    inside = (frm >= first) & (frm < first + SMOOTH)
    return np.where(inside, 1.0 / SMOOTH, 0.0).astype(ml_dtypes.bfloat16)


def nt_dot(a, b):
    return lax.dot_general(a, b, (((1,), (1,)), ((), ())), preferred_element_type=jnp.float32)


def dot(a, b):
    return jnp.dot(a, b, preferred_element_type=jnp.float32)


def whiten_kernel(first_ref, end_ref, traces_ref, wave_ref, window_ref, out_ref):
    segs, width, samples = traces_ref.shape
    pieces, groups = out_ref.shape[0], out_ref.shape[2]
    cols = segs * width
    spec = nt_dot(wave_ref[...], traces_ref[...].reshape(cols, samples))
    spec = spec.reshape(BINS // SUB, 2, SUB, cols)
    power = (spec[:, 0] * spec[:, 0] + spec[:, 1] * spec[:, 1]).reshape(BINS, cols)
    window = window_ref[...]
    high = power.astype(jnp.bfloat16)
    rest = power - high.astype(jnp.float32)
    mid = rest.astype(jnp.bfloat16)
    low = (rest - mid.astype(jnp.float32)).astype(jnp.bfloat16)
    smoothed = dot(window, high) + dot(window, mid) + dot(window, low)
    channel = lax.broadcasted_iota(jnp.int32, (BINS, cols), 1) % width
    live = (channel >= first_ref[0]) & (channel < end_ref[0])
    scaling = jnp.where(live, lax.rsqrt(smoothed + EPSILON), 0.0)
    white = spec * scaling.reshape(BINS // SUB, 1, SUB, cols)
    white = white.reshape(BINS // SUB, 2 * SUB, cols).astype(jnp.bfloat16)
    for s in range(segs):
        part = white[:, :, s * width : (s + 1) * width]
        out_ref[:, s] = part.reshape(pieces, groups, 2 * SUB, width)


def whiten(traces, live_first, live_end, pieces):
    segs, width, samples = traces.shape
    groups = BINS // SUB // pieces
    step = 2
    return pl.pallas_call(
        whiten_kernel,
        grid=(segs // step,),
        in_specs=[
            pl.BlockSpec(memory_space=pltpu.SMEM),
            pl.BlockSpec(memory_space=pltpu.SMEM),
            pl.BlockSpec((step, width, samples), lambda i: (i, 0, 0)),
            pl.BlockSpec((2 * BINS, samples), lambda i: (0, 0)),
            pl.BlockSpec((BINS, BINS), lambda i: (0, 0)),
        ],
        out_specs=pl.BlockSpec((pieces, step, groups, 2 * SUB, width), lambda i: (0, i, 0, 0, 0)),
        out_shape=jax.ShapeDtypeStruct((pieces, segs, groups, 2 * SUB, width), jnp.bfloat16),
        compiler_params=pltpu.CompilerParams(vmem_limit_bytes=40 * 2**20),
        name="whiten",
    )(live_first, live_end, traces, jnp.asarray(wave_rows()), jnp.asarray(window_rows()))


def gather_kernel(dims, mine_ref, out_ref, z_send, z_recv, x_send, x_recv, y_send, y_recv, c_send, c_recv, own_sem):
    X, Y, Z = dims
    segs = mine_ref.shape[1]
    half = segs // 2
    c = lax.axis_index("chan")
    z = lax.axis_index("seg")
    core = c % 2
    x = c // 2 % X
    y = c // 2 // X

    def chan(yy, xx, cc):
        return (yy * X + xx) * 2 + cc

    xs = [lax.rem(x + d, X) for d in range(X)]
    ys = [lax.rem(y + d, Y) for d in range(Y)]
    x_from = [lax.rem(x + X - d, X) for d in range(X)]
    y_from = [lax.rem(y + Y - d, Y) for d in range(Y)]
    zs = [lax.rem(z + d, Z) for d in range(Z)]
    z_from = [lax.rem(z + Z - d, Z) for d in range(Z)]
    sibling = chan(y, x, 1 - core)

    barrier = pltpu.get_barrier_semaphore()
    friends = [(c, zs[d]) for d in range(1, Z)]
    friends += [(chan(y, xs[d], core), z) for d in range(1, X)]
    friends += [(chan(ys[d], x, core), z) for d in range(1, Y)]
    friends += [(sibling, z)]
    for f in friends:
        pl.semaphore_signal(barrier, inc=1, device_id=f, device_id_type=MESH)
    pl.semaphore_wait(barrier, len(friends))

    started = []

    def block(owner, lo, count):
        return out_ref.at[owner, pl.ds(lo, count)]

    own = pltpu.make_async_copy(mine_ref.at[z], block(c, z * segs, segs), own_sem)
    own.start()
    for d in range(Z - 1, 0, -1):
        copy = pltpu.make_async_remote_copy(
            mine_ref.at[zs[d]], block(c, z * segs, segs), z_send.at[d], z_recv.at[d],
            device_id=(c, zs[d]), device_id_type=MESH)
        copy.start()
        started.append(copy)

    def wait_z(d):
        if d == 0:
            own.wait()
        else:
            piece = block(c, z_from[d] * segs, segs)
            pltpu.make_async_remote_copy(
                piece, piece, z_send.at[d], z_recv.at[d], device_id=(c, z_from[d]), device_id_type=MESH
            ).wait_recv()

    if Z <= 4:
        order = sorted(range(Z), key=lambda d: min(d, Z - d))
        chunks = [((d,), z_from[d] * segs, half) for d in order]
    else:
        chunks = [(tuple(range(Z)), 0, Z * half)]

    def send(ref, send_sem, recv_sem, to):
        copy = pltpu.make_async_remote_copy(
            ref, ref, send_sem, recv_sem, device_id=(to, z), device_id_type=MESH)
        copy.start()
        started.append(copy)

    def wait_recv(ref, send_sem, recv_sem):
        pltpu.make_async_remote_copy(
            ref, ref, send_sem, recv_sem, device_id=(sibling, z), device_id_type=MESH
        ).wait_recv()

    def first_hops(k):
        waits, lo, count = chunks[k]
        for d in waits:
            wait_z(d)
        a, b = block(c, lo, count), block(c, lo + count, count)
        for d in range(1, X):
            send(a, x_send.at[k, 0, 0, d], x_recv.at[k, 0, 0, d], chan(y, xs[d], core))
        for d in range(1, Y):
            send(b, y_send.at[k, 1, 0, d], y_recv.at[k, 1, 0, d], chan(ys[d], x, core))
        for d in range(1, Y):
            send(a, y_send.at[k, 0, 0, d], y_recv.at[k, 0, 0, d], chan(ys[d], x, core))
        for d in range(1, X):
            send(b, x_send.at[k, 1, 0, d], x_recv.at[k, 1, 0, d], chan(y, xs[d], core))
        for h, ref in ((0, a), (1, b)):
            send(ref, c_send.at[k, h, 0, 0], c_recv.at[k, h, 0, 0], sibling)

    def second_hops(k):
        _, lo, count = chunks[k]
        for dx in range(1, X):
            a = block(chan(y, x_from[dx], core), lo, count)
            wait_recv(a, x_send.at[k, 0, 0, dx], x_recv.at[k, 0, 0, dx])
            for d in range(1, Y):
                send(a, y_send.at[k, 0, dx, d], y_recv.at[k, 0, dx, d], chan(ys[d], x, core))
            send(a, c_send.at[k, 0, 0, dx], c_recv.at[k, 0, 0, dx], sibling)
        for dy in range(1, Y):
            b = block(chan(y_from[dy], x, core), lo + count, count)
            wait_recv(b, y_send.at[k, 1, 0, dy], y_recv.at[k, 1, 0, dy])
            for d in range(1, X):
                send(b, x_send.at[k, 1, dy, d], x_recv.at[k, 1, dy, d], chan(y, xs[d], core))
            send(b, c_send.at[k, 1, dy, 0], c_recv.at[k, 1, dy, 0], sibling)

    def last_hops(k):
        _, lo, count = chunks[k]
        for dx in range(X):
            for dy in range(1, Y):
                a = block(chan(y_from[dy], x_from[dx], core), lo, count)
                wait_recv(a, y_send.at[k, 0, dx, dy], y_recv.at[k, 0, dx, dy])
                send(a, c_send.at[k, 0, dy, dx], c_recv.at[k, 0, dy, dx], sibling)
        for dy in range(Y):
            for dx in range(1, X):
                b = block(chan(y_from[dy], x_from[dx], core), lo + count, count)
                wait_recv(b, x_send.at[k, 1, dy, dx], x_recv.at[k, 1, dy, dx])
                send(b, c_send.at[k, 1, dy, dx], c_recv.at[k, 1, dy, dx], sibling)

    n = len(chunks)
    for k in range(n + 2):
        if k < n:
            first_hops(k)
        if 0 <= k - 1 < n:
            second_hops(k - 1)
        if 0 <= k - 2 < n:
            last_hops(k - 2)
    for k in range(n):
        _, lo, count = chunks[k]
        for h in range(2):
            for dy in range(Y):
                for dx in range(X):
                    ref = block(chan(y_from[dy], x_from[dx], 1 - core), lo + h * count, count)
                    wait_recv(ref, c_send.at[k, h, dy, dx], c_recv.at[k, h, dy, dx])
    for copy in started:
        copy.wait_send()


def gather(mine, chan_count):
    Z, segs, groups, rows, width = mine.shape
    X = math.isqrt(chan_count // 2)
    Y = chan_count // 2 // X
    n = Z if Z <= 4 else 1
    m = max(X, Y)
    dma = pltpu.SemaphoreType.DMA
    return pl.pallas_call(
        partial(gather_kernel, (X, Y, Z)),
        in_specs=[pl.BlockSpec(memory_space=pl.ANY)],
        out_specs=pl.BlockSpec(memory_space=pl.ANY),
        out_shape=jax.ShapeDtypeStruct((chan_count, Z * segs, groups, rows, width), mine.dtype),
        scratch_shapes=[
            dma((Z,)), dma((Z,)),
            dma((n, 2, m, m)), dma((n, 2, m, m)),
            dma((n, 2, m, m)), dma((n, 2, m, m)),
            dma((n, 2, Y, X)), dma((n, 2, Y, X)),
            dma(()),
        ],
        compiler_params=pltpu.CompilerParams(collective_id=0, has_side_effects=True),
        name="gather",
    )(mine)


def tile_kernel(items, owner_ref, w_ref, pick_ref, mask_ref, out_ref, table, turned):
    blocks, segs, groups, rows, width = w_ref.shape
    depth = segs * rows
    part_rows = width // ROW_PARTS
    slots = table.shape[0]
    step = pl.program_id(0)

    @pl.when(step == 0)
    def _():
        me = lax.axis_index("chan")

        def clear(k, _):
            table[k] = -1
            return 0

        lax.fori_loop(0, slots, clear, 0)

        def one_row(r, n):
            for e in range(items):
                hit = owner_ref[r, e] == me

                @pl.when(hit)
                def _():
                    table[n] = r * items + e

                n = n + hit.astype(jnp.int32)
            return n

        lax.fori_loop(0, blocks, one_row, 0)

        def turn(b, _):
            for g in range(groups):
                w = w_ref[b, :, g].astype(jnp.float32).reshape(segs, 2, SUB, width)
                t = jnp.concatenate([-w[:, 1], w[:, 0]], axis=1)
                turned[b, :, g] = t.astype(jnp.bfloat16)
            return 0

        lax.fori_loop(0, blocks, turn, 0)

    code = table[step]
    r = lax.max(code, 0) // items
    e = lax.max(code, 0) % items
    t = e // ROW_PARTS
    u = e % ROW_PARTS
    real = (code >= 0) & (r + t < blocks)

    @pl.when(jnp.logical_not(real))
    def _():
        out_ref[...] = jnp.zeros_like(out_ref)

    @pl.when(real)
    def _():
        pick = pick_ref[u]
        mask = mask_ref[...]
        together = 2 if groups % 2 == 0 else 1
        for first in range(0, groups, together):
            results = []
            for g in range(first, first + together):
                w = w_ref[r, :, g].reshape(depth, width)
                spread = nt_dot(pick, w).reshape(part_rows, SUB, depth)
                left = (spread * mask[None]).reshape(part_rows * SUB, depth).astype(jnp.bfloat16)
                right = jnp.concatenate(
                    [w_ref[r + t, :, g].reshape(depth, width), turned[r + t, :, g].reshape(depth, width)],
                    axis=1,
                )
                results.append(dot(left, right).reshape(part_rows, SUB, 2 * width))
            both = jnp.concatenate(results, axis=1).astype(jnp.bfloat16)
            for i in range(part_rows):
                for a in range(2):
                    out_ref[0, 0, a, first * SUB : (first + together) * SUB, i * width : (i + 1) * width] = both[
                        i, :, a * width : (a + 1) * width
                    ]


def tiles(gathered, tile_owner):
    blocks, segs, groups, rows, width = gathered.shape
    items = tile_owner.shape[1]
    slots = 2 * items
    depth = segs * rows
    part_rows = width // ROW_PARTS
    pick = np.zeros((ROW_PARTS, part_rows * SUB, width), np.float32)
    for u in range(ROW_PARTS):
        for i in range(part_rows):
            pick[u, i * SUB : (i + 1) * SUB, u * part_rows + i] = 1.0
    mask = np.where(np.arange(depth)[None, :] % SUB == np.arange(SUB)[:, None], 1.0 / segs, 0.0)
    return pl.pallas_call(
        partial(tile_kernel, items),
        grid=(slots,),
        in_specs=[
            pl.BlockSpec(memory_space=pltpu.SMEM),
            pl.BlockSpec(gathered.shape, lambda i: (0, 0, 0, 0, 0)),
            pl.BlockSpec(pick.shape, lambda i: (0, 0, 0)),
            pl.BlockSpec(mask.shape, lambda i: (0, 0)),
        ],
        out_specs=pl.BlockSpec((1, 1, 2, groups * SUB, part_rows * width), lambda i: (0, i, 0, 0, 0)),
        out_shape=jax.ShapeDtypeStruct((1, slots, 2, groups * SUB, part_rows * width), jnp.bfloat16),
        scratch_shapes=[
            pltpu.SMEM((slots,), jnp.int32),
            pltpu.VMEM(gathered.shape, jnp.bfloat16),
        ],
        compiler_params=pltpu.CompilerParams(vmem_limit_bytes=56 * 2**20),
        name="tiles",
    )(tile_owner, gathered, jnp.asarray(pick, jnp.bfloat16), jnp.asarray(mask, jnp.float32))


def per_device(traces, live_first, live_end, tile_owner):
    white = whiten(traces, live_first, live_end, lax.axis_size("seg"))
    gathered = gather(white, lax.axis_size("chan"))
    return tiles(gathered, tile_owner)


def solution(mesh):
    placed = (P("seg", "chan", None), P("chan"), P("chan"), P())
    return jax.shard_map(
        per_device,
        mesh=mesh,
        in_specs=placed,
        out_specs=P("chan", None, None, "seg", None),
        check_vma=False,
    )
```

time: 302 us -> 51.6 us (0.17)
  the two profiles are of different devices: /device:TPU:0 before, /device:TPU:5 now
where the time goes in v1:
time: 51.6 us; the launch traced here: 50.6 us
  Pallas kernels  45.1 us (87%)
  local copies, waits for them, and re-layouts  4.13 us (8%)
  between operations  1.33 us (3%)
    pallas_call x1, Pallas kernels, gather(): pl.pallas_call(partial(gather_kernel, (X, Y, Z)), in_specs=[pl.BlockSpec(...  25.2 us
    pallas_call x1, Pallas kernels, tiles(): pl.pallas_call(partial(tile_kernel, items), grid=(slots,), in_specs=[pl.B...  18.5 us
    unnamed x8, local copies, waits for them, and re-layouts  4.13 us
    pallas_call x1, Pallas kernels, whiten(): pl.pallas_call(whiten_kernel, grid=(segs // step,), in_specs=[pl.BlockSpe...  1.5 us

profile of v1, /device:TPU:5, one launch (start us, length us, event | category | flops | bytes accessed | tf_op | source)
XLA Modules:
  0.0 50.6 jit_solution(3555168000856400290)
XLA Ops:
  1.3 0.0 copy-start
  1.3 1.5 %copy-done = bf16[4,128,1792]{2,1,0:T(8,128)(2,1)S(1)} copy-done((bf16[4,128,1792]{2,1,0:T(8,128)(2,1)S(1)}, bf16[4,128,1792]{2,1,0:T(8,128)(2,1)}, u32[]{:S(2)}) %copy-start) | copy-done | bytes 1835032
  2.8 0.0 copy-start.2
  2.8 1.2 %copy-done.2 = bf16[256,1792]{1,0:T(8,128)(2,1)S(1)} copy-done((bf16[256,1792]{1,0:T(8,128)(2,1)S(1)}, bf16[256,1792]{1,0:T(8,128)(2,1)}, u32[]{:S(2)}) %copy-start.2) | copy-done | bytes 917528
  4.0 0.0 copy-start.3
  4.0 0.8 %copy-done.3 = bf16[128,128]{1,0:T(8,128)(2,1)S(1)} copy-done((bf16[128,128]{1,0:T(8,128)(2,1)S(1)}, bf16[128,128]{1,0:T(8,128)(2,1)}, u32[]{:S(2)}) %copy-start.3) | copy-done | bytes 32792
  4.7 1.5 %whiten.1.mine_ref = bf16[4,4,4,16,128]{4,3,2,1,0:T(8,128)(2,1)S(1)} custom-call(s32[1]{0:T(128)S(6)} %copy.9.first_ref, s32[1]{0:T(128)S(6)} %copy.10.end_ref, bf16[4,128,1792]{2,1,0:T(8,128)(2,1)S(1)} %copy-done, bf16[256,1792]{1,0:T(8,128)(2,1)S(1)} %copy-done.2, bf16[128,128]{1,0:T(8,128)(2,1)S(1)} %copy-done.3), custom_call_target="tpu_custom_call" | custom-call | tf_op jit(solution)/shard_map/whiten/pallas_call | solution.py:79
  6.2 0.0 copy-start.1
  6.3 0.7 %copy-done.1 = bf16[4,4,4,16,128]{4,3,2,1,0:T(8,128)(2,1)} copy-done((bf16[4,4,4,16,128]{4,3,2,1,0:T(8,128)(2,1)}, bf16[4,4,4,16,128]{4,3,2,1,0:T(8,128)(2,1)S(1)}, u32[]{:S(2)}) %copy-start.1) | copy-done | bytes 262168
  6.9 25.2 %gather.1.w_ref = bf16[8,16,4,16,128]{4,3,2,1,0:T(8,128)(2,1)} custom-call(bf16[4,4,4,16,128]{4,3,2,1,0:T(8,128)(2,1)} %copy-done.1), custom_call_target="tpu_custom_call" | custom-call | tf_op jit(solution)/shard_map/gather/pallas_call | solution.py:236
  32.1 18.5 %tiles.1 = bf16[1,24,2,32,4096]{4,3,2,1,0:T(8,128)(2,1)} custom-call(s32[8,12]{1,0:T(8,128)} %owner_ref.1, bf16[8,16,4,16,128]{4,3,2,1,0:T(8,128)(2,1)} %gather.1.w_ref, bf16[4,256,128]{2,1,0:T(8,128)(2,1)} %constant.10.clone.pick_ref, f32[8,256]{1,0:T(8,128)} %constant.11.clone.mask_ref), custom_call_target="tpu_custom_call" | custom-call | tf_op jit(solution)/shard_map/tiles/pallas_call | solution.py:338
Async XLA Ops:
  1.3 1.5 %copy-start = (bf16[4,128,1792]{2,1,0:T(8,128)(2,1)S(1)}, bf16[4,128,1792]{2,1,0:T(8,128)(2,1)}, u32[]{:S(2)}) copy-start(bf16[4,128,1792]{2,1,0:T(8,128)(2,1)} %traces_ref.1) | copy-start | bytes 5505028
  2.8 1.2 %copy-start.2 = (bf16[256,1792]{1,0:T(8,128)(2,1)S(1)}, bf16[256,1792]{1,0:T(8,128)(2,1)}, u32[]{:S(2)}) copy-start(bf16[256,1792]{1,0:T(8,128)(2,1)} %constant.8.clone.wave_ref) | copy-start | bytes 2752516
  4.0 0.8 %copy-start.3 = (bf16[128,128]{1,0:T(8,128)(2,1)S(1)}, bf16[128,128]{1,0:T(8,128)(2,1)}, u32[]{:S(2)}) copy-start(bf16[128,128]{1,0:T(8,128)(2,1)} %constant.9.clone.window_ref) | copy-start | bytes 98308
  6.2 0.7 %copy-start.1 = (bf16[4,4,4,16,128]{4,3,2,1,0:T(8,128)(2,1)}, bf16[4,4,4,16,128]{4,3,2,1,0:T(8,128)(2,1)S(1)}, u32[]{:S(2)}) copy-start(bf16[4,4,4,16,128]{4,3,2,1,0:T(8,128)(2,1)S(1)} %whiten.1.mine_ref) | copy-start | bytes 786436
